TPU v7x, 512 devices: a whole 4x8x8 slice. The times are simulated.
512 devices in a mesh: row: 64 (over x, y, core), col: 8 (over z).
Axes of the slice: x: 4, y: 8, z: 8, core: 2. Of those that a mesh axis runs over, the one named last changes fastest.
Arguments:
- diag_block: float32 [512, 512], P('row'), as said below
- panel: float32 [256, 256, 512], P('row', 'col'), may hold values from -1.5 to 1.5
- panel_mask: int32 [256, 2], P('row'), may hold values 0 or 1
- slot_rows: int32 [64, 4, 16], replicated, may hold values from -1 to 255, as said below
- trail: float32 [256, 16, 256, 256], P('row', None, 'col'), may hold values from -6 to 6
Outputs:
- diag_factor: float32 [512, 512], P('row')
- panel_factor: float32 [256, 256, 512], P('row', 'col')
- trail_out: float32 [256, 16, 256, 256], P('row', None, 'col')
Inputs may be any that keep to these rules, and one draw needn't show every extreme that they name: For each r and t, the entries slot_rows[r, t, :] that are not -1 come first and are distinct. For each r, all entries that lie in the tile rows r2 * 4 to r2 * 4 + 3 of one index r2 of row name the same tile row. In every draw some r has no entry -1. `diag_block`: Symmetric; every diagonal entry exceeds the sum of magnitudes of the other entries of its row.
All inputs are finite; a program needn't handle non-finite values. No bound on the sum of `panel_mask` on one device may be relied on, other than what follows from the above.
Results may differ from a plain program's by a relative error of at most 0.0003.
Values sent between devices are 32-bit elements; how exact they have to be, the bound alone decides.
A program may use at most 64 MiB of HBM per device.

v0:
```python
import jax
import jax.numpy as jnp
from jax import lax
from jax.experimental import pallas as pl
from jax.experimental.pallas import tpu as pltpu
from jax.sharding import PartitionSpec as P

MESH = pl.DeviceIdType.MESH
HI = lax.Precision.HIGHEST
NX, NY, NK, NZ = 4, 8, 2, 8
TILES, SLAB, WIDTH, TW = 4, 32, 512, 256
RB, RA = 24, 8
SLOTS = 16


def dot32(a, b, tb=False):
    dims = (((1,), (1 if tb else 0,)), ((), ()))
    return lax.dot_general(a, b, dims, precision=HI, preferred_element_type=jnp.float32)


def dot16(a, b):
    dims = (((1,), (1,)), ((), ()))
    return lax.dot_general(a, b, dims, preferred_element_type=jnp.float32)


def split(x):
    hi = x.astype(jnp.bfloat16)
    lo = (x - hi.astype(jnp.float32)).astype(jnp.bfloat16)
    return hi, lo


def lanes(x, lane):
    return jnp.broadcast_to(x[:, lane : lane + 1], x.shape)


def rows(x, row):
    return jnp.broadcast_to(x[row : row + 1, :], (8, 128))


def total(xs):
    while len(xs) > 1:
        xs = [xs[i] + xs[i + 1] if i + 1 < len(xs) else xs[i] for i in range(0, len(xs), 2)]
    return xs[0]


def pivot8(cols):
    d, low, rs, inv = {}, {}, {}, {}
    for b in range(8):
        for a in range(b, 8):
            d[a, b] = rows(cols[b], a)
    for k in range(8):
        rs[k] = lax.rsqrt(d[k, k])
        for i in range(k + 1, 8):
            low[i, k] = d[i, k] * rs[k]
        for i in range(k + 1, 8):
            for j in range(k + 1, i + 1):
                d[i, j] = d[i, j] - low[i, k] * low[j, k]
        inv[k, k] = rs[k]
        for m in range(k):
            s = low[k, m] * inv[m, m]
            for q in range(m + 1, k):
                s = s + low[k, q] * inv[q, m]
            inv[k, m] = -(rs[k] * s)
    return inv


def sweep8(j, m_ref, lt_ref):
    r0 = j * 8
    sub = lax.broadcasted_iota(jnp.int32, (8, 128), 0)
    lane = lax.broadcasted_iota(jnp.int32, (8, 128), 1)
    block = m_ref[r0 : r0 + 8, :]
    inv = pivot8([lanes(block, r0 + b) for b in range(8)])
    zero = jnp.zeros((8, 128), jnp.float32)
    colv, rowv = [], []
    for m in range(8):
        v = zero
        for k in range(m, 8):
            v = jnp.where(sub == k, inv[k, m], v)
        colv.append(v)
    for k in range(8):
        v = zero
        for m in range(k + 1):
            v = jnp.where(sub == m, inv[k, m], v)
        rowv.append(v)
    inside = (lane >= r0) & (lane < r0 + 8)
    u = total([colv[m] * rows(block, m) for m in range(8)])
    lt_ref[r0 : r0 + 8, :] = jnp.where(lane >= r0 + sub, u, 0.0)
    pattern = zero
    for m in range(8):
        pattern = jnp.where(lane == r0 + m, colv[m], pattern)
    u = jnp.where(inside, pattern, u)
    p = total([rowv[k] * rows(u, k) for k in range(8)])
    spread = [rows(p, m) for m in range(8)]
    m_ref[r0 : r0 + 8, :] = u
    for i in range(j + 1, 16):
        mi = m_ref[8 * i : 8 * i + 8, :]
        upd = total([lanes(mi, r0 + m) * spread[m] for m in range(8)])
        m_ref[8 * i : 8 * i + 8, :] = jnp.where(inside, 0.0, mi) - upd


def block_update(J, a_ref, lt_ref, blk, ltb):
    r0, r1 = J * 128, J * 128 + 128
    tri = lax.broadcasted_iota(jnp.int32, (128, 128), 0) >= lax.broadcasted_iota(jnp.int32, (128, 128), 1)
    linv = jnp.where(tri, blk[...], 0.0)
    lt_ref[r0:r1, r0:r1] = ltb[...]
    if J > 0:
        lt_ref[r0:r1, :r0] = jnp.zeros((128, r0), jnp.float32)
        uw = dot32(linv, a_ref[r0:r1, :r0])
        a_ref[r0:r1, :r0] = uw
    if J < 3:
        lcol = dot32(a_ref[r1:, r0:r1], linv, tb=True)
        ut = dot32(linv, a_ref[r0:r1, r1:])
        lt_ref[r0:r1, r1:] = ut
        a_ref[r1:, r1:] = a_ref[r1:, r1:] - dot32(lcol, ut)
        a_ref[r1:, r0:r1] = -dot32(lcol, linv)
        if J > 0:
            a_ref[r1:, :r0] = a_ref[r1:, :r0] - dot32(lcol, uw)
        a_ref[r0:r1, r1:] = jnp.zeros((128, 512 - r1), jnp.float32)
    a_ref[r0:r1, r0:r1] = linv


def kernel(
    diag_ref, panel_ref, mask_ref, table_ref, slot_ref, trail_ref,
    factor_ref, solved_ref, out_ref,
    a5, w, lt, blk, ltb, xa, zg, yb0, yb1, yb2, yb3, yb4, yb5, yb6, yb7,
    sb, sa, pb, pa, bhi, blo, lhi, llo, trail_v, out_v,
    dy_s, dy_r, dx_s, dx_r, dk_s, dk_r, xa_s, xa_r, z_s, z_r, y_s, y_r, sb_s, sb_r, sa_s, sa_r, t_sem, o_sem,
):
    me = lax.axis_index("row")
    z = lax.axis_index("col")
    x, y, k = me // 16, (me // 2) % 8, me % 2

    def dev(dx=0, dy=0, dk=0, dz=0):
        return (((x + dx) % 4 * 8 + (y + dy) % 8) * 2 + (k + dk) % 2, (z + dz) % 8)

    def remote(src, dst, ss, rs, to):
        return pltpu.make_async_remote_copy(src, dst, ss, rs, device_id=to, device_id_type=MESH)

    trail_in = [
        pltpu.make_async_copy(trail_ref.at[t], trail_v.at[t], t_sem.at[t]) for t in range(TILES)
    ]
    for c in trail_in:
        c.start()

    first_half = lax.broadcasted_iota(jnp.int32, (SLAB, WIDTH), 1) < TW
    for t in range(TILES):
        keep = jnp.where(first_half, mask_ref[t, 0].astype(jnp.float32), mask_ref[t, 1].astype(jnp.float32))
        v = panel_ref[t] * keep
        zg[t, pl.ds(z, 1)] = v[None]
        yb0[t] = v[:RB]
        xa[pl.ds(x, 1), t] = v[RB:][None]
    a5[pl.ds(x, 1), pl.ds(y, 1), pl.ds(k, 1)] = diag_ref[...][None, None, None]

    barrier = pltpu.get_barrier_semaphore()
    partners = [dev(dz=1), dev(dz=-1)]
    partners += [dev(dx=e // 2, dk=e % 2) for e in range(1, 8)]
    partners += [dev(dy=e // 2, dk=e % 2) for e in range(2, 16)]
    for to in partners:
        pl.semaphore_signal(barrier, inc=1, device_id=to, device_id_type=MESH)
    pl.semaphore_wait(barrier, len(partners))

    def dy_copy(i):
        return remote(diag_ref, a5.at[x, y, k], dy_s.at[i], dy_r.at[i], dev(dy=i + 1))

    def dx_copy(c, i):
        ref = a5.at[x, :, k, :, pl.ds(c * 128, 128)]
        return remote(ref, ref, dx_s.at[c, i], dx_r.at[c, i], dev(dx=i + 1))

    def dk_copy(c):
        ref = a5.at[:, :, k, :, pl.ds(c * 128, 128)]
        return remote(ref, ref, dk_s.at[c], dk_r.at[c], dev(dk=1))

    for i in range(7):
        dy_copy(i).start()

    yb = [yb0, yb1, yb2, yb3, yb4, yb5, yb6, yb7]
    step_of = {0: 0, 1: -1, 2: -2, 3: -3, 4: 1, 5: 2, 6: 3, 7: 4}

    def ring(step, way):
        src = 0 if step == 0 else (step if way == 0 else step + 3)
        dst = 7 if step == 3 else (step + 1 if way == 0 else step + 4)
        part = pl.ds(0, TILES) if step < 3 else pl.ds(2 * way, 2)
        return src, dst, part

    def z_copy(step, way):
        src, _, part = ring(step, way)
        block = (z + step_of[src]) % 8
        ref = zg.at[part, block]
        return remote(ref, ref, z_s.at[step, way], z_r.at[step, way], dev(dz=1 if way == 0 else -1))

    def y_copy(step, way):
        src, dst, part = ring(step, way)
        return remote(
            yb[src].at[part], yb[dst].at[part], y_s.at[step, way], y_r.at[step, way],
            dev(dy=1 if way == 0 else -1),
        )

    def xa_copy(i):
        return remote(xa.at[x], xa.at[x], xa_s.at[i], xa_r.at[i], dev(dx=i + 1))

    for way in range(2):
        z_copy(0, way).start()
        y_copy(0, way).start()
    for i in range(3):
        xa_copy(i).start()

    def sb_copy(pos, e, yy):
        return remote(
            sb.at[e, pos], pb.at[x, k, yy], sb_s.at[e, pos], sb_r.at[e, pos],
            dev(dx=(e + 1) // 2, dk=(e + 1) % 2),
        )

    def send_block(pos):
        yy = (y + step_of[pos]) % 8
        source = (x * 8 + yy) * 2 + k
        buf = yb[pos]
        pb[x, k, yy] = buf[table_ref[me, source]]

        def body(e, c):
            to = dev(dx=(e + 1) // 2, dk=(e + 1) % 2)[0]
            sb[e, pos] = buf[table_ref[to, source]]
            sb_copy(pos, e, yy).start()
            return c

        lax.fori_loop(0, 7, body, 0)

    def sa_copy(e):
        return remote(
            sa.at[e], pa.at[y, k], sa_s.at[e], sa_r.at[e], dev(dy=(e + 1) // 2, dk=(e + 1) % 2)
        )

    def send_cross():
        for xx in range(NX):
            pa[y, k, xx] = xa[xx, table_ref[me, (xx * 8 + y) * 2 + k]]

        def body(e, c):
            to = dev(dy=(e + 1) // 2, dk=(e + 1) % 2)[0]
            for xx in range(NX):
                sa[e, xx] = xa[xx, table_ref[to, (xx * 8 + y) * 2 + k]]
            sa_copy(e).start()
            return c

        lax.fori_loop(0, 15, body, 0)

    def service(step):
        for way in range(2):
            y_copy(step, way).wait_recv()
            if step < 3:
                y_copy(step + 1, way).start()
        for way in range(2):
            z_copy(step, way).wait_recv()
            if step < 3:
                z_copy(step + 1, way).start()
        if step < 3:
            send_block(step + 1)
            send_block(step + 4)
        else:
            send_block(7)

    for i in range(7):
        dy_copy(i).wait_recv()
    for c in range(4):
        for i in range(3):
            dx_copy(c, i).start()
    send_block(0)
    for i in range(3):
        xa_copy(i).wait_recv()
    send_cross()
    for c in range(4):
        for i in range(3):
            dx_copy(c, i).wait_recv()
        dk_copy(c).start()
    for c in range(4):
        dk_copy(c).wait_recv()
    for xx in range(NX):
        w[xx * 128 : xx * 128 + 128, :] = a5[xx].reshape(128, 512)
    service(0)

    def factor_block(J, carry):
        r0 = pl.multiple_of(J * 128, 128)
        blk[...] = w[pl.ds(r0, 128), pl.ds(r0, 128)]
        for j in range(16):
            sweep8(j, blk, ltb)
        for s in range(4):

            @pl.when(J == s)
            def _(s=s):
                block_update(s, w, lt, blk, ltb)
                if s < 3:
                    service(s + 1)

        return carry

    lax.fori_loop(0, 4, factor_block, 0)

    pick = lax.broadcasted_iota(jnp.int32, (8, 512), 1) == me * 8 + lax.broadcasted_iota(jnp.int32, (8, 512), 0)
    factor_ref[...] = dot32(pick.astype(jnp.float32), lt[...], tb=True)
    own = zg[:, pl.ds(z, 1)].reshape(TILES * SLAB, WIDTH)
    solved_ref[...] = dot32(own, w[...], tb=True).reshape(TILES, SLAB, WIDTH)
    wv = w[...]
    lt[...] = lax.dot_general(
        wv, wv, (((0,), (0,)), ((), ())), precision=HI, preferred_element_type=jnp.float32
    )
    for t in range(TILES):
        bhi[t], blo[t] = split(dot32(zg[t].reshape(TW, WIDTH), lt[...]))

    for pos in range(8):
        yy = (y + step_of[pos]) % 8
        for e in range(7):
            sb_copy(pos, e, yy).wait_recv()
    for e in range(15):
        sa_copy(e).wait_recv()

    def update(t, carry):
        live = []
        for s in range(SLOTS):
            p = slot_ref[t, s]
            live.append((p >= 0).astype(jnp.float32))
            src = jnp.maximum(p, 0) // TILES
            x2, y2, k2 = src // 16, (src // 2) % 8, src % 2
            v = jnp.concatenate([pb[x2, k2, y2], pa[y2, k2, x2]], axis=0)
            hi, lo = split(v)
            lhi[s * SLAB : s * SLAB + SLAB, :] = hi
            llo[s * SLAB : s * SLAB + SLAB, :] = lo
        bh, bl = bhi[t], blo[t]
        upd = dot16(lhi[...], bh) + (dot16(lhi[...], bl) + dot16(llo[...], bh))
        pltpu.make_async_copy(trail_ref.at[t], trail_v.at[t], t_sem.at[t]).wait()
        for s in range(SLOTS):
            out_v[t, s] = trail_v[t, s] - upd[s * SLAB : s * SLAB + SLAB] * live[s]
        pltpu.make_async_copy(out_v.at[t], out_ref.at[t], o_sem.at[t]).start()
        return carry

    lax.fori_loop(0, TILES, update, 0)

    for i in range(7):
        dy_copy(i).wait_send()
    for c in range(4):
        for i in range(3):
            dx_copy(c, i).wait_send()
        dk_copy(c).wait_send()
    for i in range(3):
        xa_copy(i).wait_send()
    for step in range(4):
        for way in range(2):
            z_copy(step, way).wait_send()
            y_copy(step, way).wait_send()
    for pos in range(8):
        yy = (y + step_of[pos]) % 8
        for e in range(7):
            sb_copy(pos, e, yy).wait_send()
    for e in range(15):
        sa_copy(e).wait_send()
    for t in range(TILES):
        pltpu.make_async_copy(out_v.at[t], out_ref.at[t], o_sem.at[t]).wait()


def per_device(diag_block, panel, panel_mask, slot_rows, trail):
    n_row = slot_rows.shape[0]
    me = lax.axis_index("row")
    slots = slot_rows.reshape(n_row, -1)
    match = (slots >> 2)[:, :, None] == jnp.arange(n_row, dtype=jnp.int32)
    table = jnp.max(jnp.where(match, (slots & 3)[:, :, None], 0), axis=1)
    my_slots = lax.dynamic_index_in_dim(slot_rows, me, 0, keepdims=False)
    f32 = jnp.float32
    vm = lambda *shape: pltpu.VMEM(shape, f32)
    dma = lambda *shape: pltpu.SemaphoreType.DMA(shape)
    bf = lambda *shape: pltpu.VMEM(shape, jnp.bfloat16)
    vmem = pl.BlockSpec(memory_space=pltpu.VMEM)
    smem = pl.BlockSpec(memory_space=pltpu.SMEM)
    hbm = pl.BlockSpec(memory_space=pl.ANY)
    return pl.pallas_call(
        kernel,
        out_shape=(
            jax.ShapeDtypeStruct(diag_block.shape, f32),
            jax.ShapeDtypeStruct(panel.shape, f32),
            jax.ShapeDtypeStruct(trail.shape, f32),
        ),
        in_specs=[vmem, vmem, smem, smem, smem, hbm],
        out_specs=(vmem, vmem, hbm),
        scratch_shapes=[
            vm(NX, NY, NK, 8, WIDTH), vm(512, 512), vm(512, 512), vm(128, 128), vm(128, 128),
            vm(NX, TILES, RA, WIDTH), vm(TILES, NZ, SLAB, WIDTH),
            *[vm(TILES, RB, WIDTH) for _ in range(8)],
            vm(7, 8, RB, WIDTH), vm(15, NX, RA, WIDTH),
            vm(NX, NK, NY, RB, WIDTH), vm(NY, NK, NX, RA, WIDTH),
            bf(TILES, TW, WIDTH), bf(TILES, TW, WIDTH), bf(SLOTS * SLAB, WIDTH), bf(SLOTS * SLAB, WIDTH),
            vm(TILES, SLOTS, SLAB, TW), vm(TILES, SLOTS, SLAB, TW),
            dma(7), dma(7), dma(4, 3), dma(4, 3), dma(4), dma(4), dma(3), dma(3),
            dma(4, 2), dma(4, 2), dma(4, 2), dma(4, 2), dma(7, 8), dma(7, 8), dma(15), dma(15),
            dma(4), dma(4),
        ],
        compiler_params=pltpu.CompilerParams(
            collective_id=0, has_side_effects=True, vmem_limit_bytes=56 * 1024 * 1024
        ),
        name="panels",
    )(diag_block, panel, panel_mask, table, my_slots, trail)


def solution(mesh):
    in_specs = (
        P("row", None),
        P("row", "col", None),
        P("row", None),
        P(),
        P("row", None, "col", None),
    )
    out_specs = (P("row", None), P("row", "col", None), P("row", None, "col", None))
    return jax.shard_map(
        per_device, mesh=mesh, in_specs=in_specs, out_specs=out_specs, check_vma=False
    )
```

profile of v0, /device:TPU:1, one launch (start us, length us, event | category | flops | bytes accessed | tf_op | source)
XLA Modules:
  0.0 97.0 jit_solution(9740051283012827114)
XLA Ops:
  0.6 1.6 %dynamic-slice_reduce_fusion.slot_ref = s32[4,16]{1,0:T(4,128)} fusion(s32[64,4,16]{0,2,1:T(8,128)} %param.8, s32[]{:T(128)S(6)} %select_n.9), kind=kLoop, calls=%fused_computation.2 | loop fusion | bytes 516 | tf_op jit(solution)/shard_map/jit(dynamic_index_in_dim)/dynamic_slice | solution.py:363
  2.2 1.3 %copy.16.mask_ref = s32[4,2]{1,0:T(4,128)} copy(s32[4,2]{0,1:T(2,128)} %param.7) | data formatting | bytes 64 | tf_op args[2]
  3.5 0.8 broadcast_shift-right-arithmetic_fusion
  4.3 0.1 copy.14
  4.4 0.1 copy.15
  4.4 2.0 %select_reduce_fusion.table_ref = s32[64,64]{1,0:T(8,128)} fusion(s32[64,64]{1,0:T(8,128)S(1)} %copy.15, s32[64,64]{1,0:T(8,128)S(1)} %copy.14), kind=kLoop, calls=%fused_computation | loop fusion | flops 782336 | bytes 49152 | tf_op jit(solution)/shard_map/reduce_max | solution.py:362
  6.5 84.4 %panels.1 = (f32[8,512]{1,0:T(8,128)}, f32[4,32,512]{2,1,0:T(8,128)}, f32[4,16,32,256]{3,2,1,0:T(8,128)}) custom-call(f32[8,512]{1,0:T(8,128)} %diag_ref.1, f32[4,32,512]{2,1,0:T(8,128)} %panel_ref.1, s32[4,2]{1,0:T(4,128)} %copy.16.mask_ref, s32[64,64]{1,0:T(8,128)} %select_reduce_fusion.table_ref, s32[4,16]{1,0:T(4,128)} %dynamic-slice_reduce_fusion.slot_ref, ...), custom_call_target="tpu_custom_call" | custom-call | tf_op jit(solution)/shard_map/panels/pallas_call | solution.py:371
  90.8 1.3 %copy.20 = f32[8,512]{1,0:T(8,128)} copy(f32[8,512]{1,0:T(8,128)} %get-tuple-element.8) | data formatting | bytes 32768
  92.2 1.7 %copy.21 = f32[4,32,512]{2,1,0:T(8,128)} copy(f32[4,32,512]{2,1,0:T(8,128)} %get-tuple-element.9) | data formatting | bytes 524288
  93.8 3.2 %copy.22 = f32[4,16,32,256]{3,2,1,0:T(8,128)} copy(f32[4,16,32,256]{3,2,1,0:T(8,128)} %get-tuple-element.10) | data formatting | bytes 4194304
where the time goes:
time: 97.4 us; the launch traced here: 97 us
  Pallas kernels  84.4 us (87%)
  local copies, waits for them, and re-layouts  9.2 us (9%)
  other arithmetic  2.79 us (3%)
    pallas_call x1, Pallas kernels, per_device(): pl.pallas_call(kernel, out_shape=(jax.ShapeDtypeStruct(diag_block.shape,...  84.4 us
    unnamed x4, local copies, waits for them, and re-layouts  7.49 us
    reduce_max x1, other arithmetic, per_device(): table = jnp.max(jnp.where(match, (slots & 3)[:, :, None], 0), axis=1)  2.03 us

commit v1 on v0

v1 whole, which is shorter than its diff:
```python
import jax
import jax.numpy as jnp
from jax import lax
from jax.experimental import pallas as pl
from jax.experimental.pallas import tpu as pltpu
from jax.sharding import PartitionSpec as P

MESH = pl.DeviceIdType.MESH
HI = lax.Precision.HIGHEST
NX, NY, NK, NZ = 4, 8, 2, 8
TILES, SLAB, WIDTH, TW = 4, 32, 512, 256
RB, RA = 24, 8
SLOTS = 16


def dot32(a, b, tb=False):
    dims = (((1,), (1 if tb else 0,)), ((), ()))
    return lax.dot_general(a, b, dims, precision=HI, preferred_element_type=jnp.float32)


def dot16(a, b):
    dims = (((1,), (1,)), ((), ()))
    return lax.dot_general(a, b, dims, preferred_element_type=jnp.float32)


def split(x):
    hi = x.astype(jnp.bfloat16)
    lo = (x - hi.astype(jnp.float32)).astype(jnp.bfloat16)
    return hi, lo


def dot48(a, b, tb=False):
    dims = (((1,), (1 if tb else 0,)), ((), ()))
    ah, al = split(a)
    bh, bl = split(b)
    dot = lambda p, q: lax.dot_general(p, q, dims, preferred_element_type=jnp.float32)
    return dot(ah, bh) + (dot(ah, bl) + dot(al, bh))


def lanes(x, lane):
    return jnp.broadcast_to(x[:, lane : lane + 1], x.shape)


def rows(x, row):
    return jnp.broadcast_to(x[row : row + 1, :], (8, 128))


def total(xs):
    while len(xs) > 1:
        xs = [xs[i] + xs[i + 1] if i + 1 < len(xs) else xs[i] for i in range(0, len(xs), 2)]
    return xs[0]


def pivot8(cols):
    d, low, rs, inv = {}, {}, {}, {}
    for b in range(8):
        for a in range(b, 8):
            d[a, b] = rows(cols[b], a)
    for k in range(8):
        rs[k] = lax.rsqrt(d[k, k])
        for i in range(k + 1, 8):
            low[i, k] = d[i, k] * rs[k]
        for i in range(k + 1, 8):
            for j in range(k + 1, i + 1):
                d[i, j] = d[i, j] - low[i, k] * low[j, k]
        inv[k, k] = rs[k]
        for m in range(k):
            s = low[k, m] * inv[m, m]
            for q in range(m + 1, k):
                s = s + low[k, q] * inv[q, m]
            inv[k, m] = -(rs[k] * s)
    return inv


def sweep8(j, m_ref, lt_ref):
    r0 = j * 8
    sub = lax.broadcasted_iota(jnp.int32, (8, 128), 0)
    lane = lax.broadcasted_iota(jnp.int32, (8, 128), 1)
    block = m_ref[r0 : r0 + 8, :]
    inv = pivot8([lanes(block, r0 + b) for b in range(8)])
    zero = jnp.zeros((8, 128), jnp.float32)
    colv, rowv = [], []
    for m in range(8):
        v = zero
        for k in range(m, 8):
            v = jnp.where(sub == k, inv[k, m], v)
        colv.append(v)
    for k in range(8):
        v = zero
        for m in range(k + 1):
            v = jnp.where(sub == m, inv[k, m], v)
        rowv.append(v)
    inside = (lane >= r0) & (lane < r0 + 8)
    u = total([colv[m] * rows(block, m) for m in range(8)])
    lt_ref[r0 : r0 + 8, :] = jnp.where(lane >= r0 + sub, u, 0.0)
    pattern = zero
    for m in range(8):
        pattern = jnp.where(lane == r0 + m, colv[m], pattern)
    u = jnp.where(inside, pattern, u)
    p = total([rowv[k] * rows(u, k) for k in range(8)])
    spread = [rows(p, m) for m in range(8)]
    m_ref[r0 : r0 + 8, :] = u
    for i in range(j + 1, 16):
        mi = m_ref[8 * i : 8 * i + 8, :]
        upd = total([lanes(mi, r0 + m) * spread[m] for m in range(8)])
        m_ref[8 * i : 8 * i + 8, :] = jnp.where(inside, 0.0, mi) - upd


def block_update(J, a_ref, lt_ref, blk, ltb):
    r0, r1 = J * 128, J * 128 + 128
    tri = lax.broadcasted_iota(jnp.int32, (128, 128), 0) >= lax.broadcasted_iota(jnp.int32, (128, 128), 1)
    linv = jnp.where(tri, blk[...], 0.0)
    lt_ref[r0:r1, r0:r1] = ltb[...]
    if J > 0:
        uw = dot32(linv, a_ref[r0:r1, :r0])
        a_ref[r0:r1, :r0] = uw
    if J < 3:
        lcol = dot32(a_ref[r1:, r0:r1], linv, tb=True)
        ut = lcol.T
        lt_ref[r0:r1, r1:] = ut
        a_ref[r1:, r1:] = a_ref[r1:, r1:] - dot32(lcol, ut)
        a_ref[r1:, r0:r1] = -dot32(lcol, linv)
        if J > 0:
            a_ref[r1:, :r0] = a_ref[r1:, :r0] - dot32(lcol, uw)
    a_ref[r0:r1, r0:r1] = linv
    if J < 3:
        a_ref[r0:r1, r1:] = jnp.zeros((128, 512 - r1), jnp.float32)


def kernel(
    diag_ref, panel_ref, mask_ref, slots_ref, trail_ref,
    factor_ref, solved_ref, out_ref,
    a7, w, lt, blk, ltb, xa, zg, yb0, yb1, yb2, yb3, yb4, yb5, yb6, yb7,
    sb, sa, pb, pa, bhi, blo, ph, pll, trail_v, out_v, panel_v, mask_v, slots_v, slots_s, table_v, table_s,
    dy_s, dy_r, dx_s, dx_r, dk_s, dk_r, xa_s, xa_r, z_s, z_r, y_s, y_r, sb_s, sb_r, sa_s, sa_r, l_sem, t_sem, o_sem,
):
    me = lax.axis_index("row")
    z = lax.axis_index("col")
    x, y, k = me // 16, (me // 2) % 8, me % 2

    def dev(dx=0, dy=0, dk=0, dz=0):
        return (((x + dx) % 4 * 8 + (y + dy) % 8) * 2 + (k + dk) % 2, (z + dz) % 8)

    def remote(src, dst, ss, rs, to):
        return pltpu.make_async_remote_copy(src, dst, ss, rs, device_id=to, device_id_type=MESH)

    loads = [
        pltpu.make_async_copy(diag_ref.at[:, pl.ds(c * 128, 128)], a7.at[c, k, x, y], l_sem.at[c])
        for c in range(4)
    ]
    loads += [
        pltpu.make_async_copy(panel_ref, panel_v, l_sem.at[4]),
        pltpu.make_async_copy(mask_ref, mask_v, l_sem.at[5]),
        pltpu.make_async_copy(slots_ref, slots_v, l_sem.at[6]),
        pltpu.make_async_copy(slots_ref, slots_s, l_sem.at[8]),
    ]
    for c in loads:
        c.start()
    trail_in = [pltpu.make_async_copy(trail_ref.at[t], trail_v.at[t], t_sem.at[t]) for t in range(TILES)]
    trail_out = [pltpu.make_async_copy(out_v.at[t], out_ref.at[t], o_sem.at[t]) for t in range(TILES)]

    barrier = pltpu.get_barrier_semaphore()
    partners = [dev(dz=1), dev(dz=-1)]
    partners += [dev(dx=e // 2, dk=e % 2) for e in range(1, 8)]
    partners += [dev(dy=e // 2, dk=e % 2) for e in range(2, 16)]
    for to in partners:
        pl.semaphore_signal(barrier, inc=1, device_id=to, device_id_type=MESH)
    for c in loads[:6]:
        c.wait()

    first_half = lax.broadcasted_iota(jnp.int32, (SLAB, WIDTH), 1) < TW
    mask = mask_v[...].astype(jnp.float32)
    for t in range(TILES):
        keep = jnp.where(
            first_half,
            jnp.broadcast_to(mask[0:1, t : t + 1], (SLAB, WIDTH)),
            jnp.broadcast_to(mask[1:2, t : t + 1], (SLAB, WIDTH)),
        )
        v = panel_v[t] * keep
        zg[t, pl.ds(z, 1)] = v[None]
        yb0[t] = v[:RB]
        xa[pl.ds(x, 1), t] = v[RB:][None]
    pl.semaphore_wait(barrier, len(partners))

    def dy_copy(c, i):
        ref = a7.at[c, k, x, y]
        return remote(ref, ref, dy_s.at[c], dy_r.at[c], dev(dy=i + 1))

    def dx_copy(c, i):
        ref = a7.at[c, k, x]
        return remote(ref, ref, dx_s.at[c], dx_r.at[c, i], dev(dx=i + 1))

    def dy_all(c):
        ref = a7.at[c, k, x, pl.ds(0, 7)]
        return remote(ref, ref, dy_s.at[c], dy_r.at[c], dev(dy=1))

    def dx_all(c):
        ref = a7.at[c, k, pl.ds(0, 3)]
        return remote(ref, ref, dx_s.at[c], dx_r.at[c, 0], dev(dx=1))

    def dk_copy(c):
        ref = a7.at[c, k, pl.ds(c, 4 - c)]
        return remote(ref, ref, dk_s.at[c], dk_r.at[c], dev(dk=1))

    def start_dy(c):
        @pl.when(x >= c)
        def _():
            for i in range(7):
                dy_copy(c, i).start()

    start_dy(0)

    yb = [yb0, yb1, yb2, yb3, yb4, yb5, yb6, yb7]
    step_of = {0: 0, 1: -1, 2: -2, 3: -3, 4: 1, 5: 2, 6: 3, 7: 4}

    def ring(step, way):
        src = 0 if step == 0 else (step if way == 0 else step + 3)
        dst = 7 if step == 3 else (step + 1 if way == 0 else step + 4)
        part = pl.ds(0, TILES) if step < 3 else pl.ds(2 * way, 2)
        return src, dst, part

    def z_copy(step, way):
        src, _, part = ring(step, way)
        block = (z + step_of[src]) % 8
        ref = zg.at[part, block]
        return remote(ref, ref, z_s.at[step, way], z_r.at[step, way], dev(dz=1 if way == 0 else -1))

    def y_copy(step, way):
        src, dst, part = ring(step, way)
        return remote(
            yb[src].at[part], yb[dst].at[part], y_s.at[step, way], y_r.at[step, way],
            dev(dy=1 if way == 0 else -1),
        )

    def xa_copy(i):
        return remote(xa.at[x], xa.at[x], xa_s, xa_r, dev(dx=i + 1))

    xa_all = remote(xa.at[pl.ds(0, 3)], xa.at[pl.ds(0, 3)], xa_s, xa_r, dev(dx=1))
    for way in range(2):
        y_copy(0, way).start()
    for c in range(1, 4):
        start_dy(c)
    for i in range(3):
        xa_copy(i).start()
    for way in range(2):
        z_copy(0, way).start()

    loads[6].wait()
    wanted = slots_v[...].reshape(TILES * SLOTS, 64)
    source_row, tile = wanted >> 2, wanted & 3
    sub16 = lax.broadcasted_iota(jnp.int32, (16, 64), 0)
    table = jnp.zeros((16, 64), jnp.int32)
    for i in range(12):
        src = (x * 8 + i) * 2 + k if i < 8 else ((i - 8) * 8 + y) * 2 + k
        best = jnp.max(jnp.where(source_row == src, tile, 0), axis=0, keepdims=True)
        table = jnp.where(sub16 == i, best, table)
    table_v[...] = table
    to_scalar = pltpu.make_async_copy(table_v, table_s, l_sem.at[7])
    to_scalar.start()

    def sb_copy(pos, e, yy):
        return remote(
            sb.at[e, pos], pb.at[x, k, yy], sb_s, sb_r.at[pos],
            dev(dx=(e + 1) // 2, dk=(e + 1) % 2),
        )

    def send_block(pos):
        yy = (y + step_of[pos]) % 8
        buf = yb[pos]
        pb[x, k, yy] = buf[table_s[yy, me]]

        def body(e, c):
            to = dev(dx=(e + 1) // 2, dk=(e + 1) % 2)[0]
            sb[e, pos] = buf[table_s[yy, to]]
            sb_copy(pos, e, yy).start()
            return c

        lax.fori_loop(0, 7, body, 0)

    def sa_copy(e):
        return remote(
            sa.at[e], pa.at[y, k], sa_s, sa_r.at[(e + 1) // 2], dev(dy=(e + 1) // 2, dk=(e + 1) % 2)
        )

    def send_cross(lo, hi):
        def body(e, c):
            to = dev(dy=(e + 1) // 2, dk=(e + 1) % 2)[0]
            for xx in range(NX):
                sa[e, xx] = xa[xx, table_s[8 + xx, to]]
            sa_copy(e).start()
            return c

        lax.fori_loop(lo, hi, body, 0)

    def service(step):
        for way in range(2):
            y_copy(step, way).wait_recv()
            if step < 3:
                y_copy(step + 1, way).start()
        for way in range(2):
            z_copy(step, way).wait_recv()
            if step < 3:
                z_copy(step + 1, way).start()
        if step < 3:
            send_block(step + 1)
            send_block(step + 4)
        else:
            send_block(7)
        send_cross(4 * step, min(4 * step + 4, 15))

    def turn_diag(c):
        @pl.when(x >= c)
        def _():
            dy_all(c).wait_recv()
            for i in range(3):
                dx_copy(c, i).start()

    def pass_diag(c):
        for i in range(3):

            @pl.when((x + 3 - i) % 4 >= c)
            def _(i=i):
                dx_copy(c, i).wait_recv()

        dk_copy(c).start()

    def unpack(c):
        dk_copy(c).wait_recv()
        for xx in range(c, NX):
            v = jnp.stack([a7[c, 0, xx], a7[c, 1, xx]], axis=1)
            w[xx * 128 : xx * 128 + 128, c * 128 : c * 128 + 128] = v.reshape(128, 128)

    w[...] = jnp.zeros_like(w)
    lt[...] = jnp.zeros_like(lt)
    for c in range(4):
        turn_diag(c)
    to_scalar.wait()
    send_block(0)
    xa_all.wait_recv()
    for xx in range(NX):
        pa[y, k, xx] = xa[xx, table_s[8 + xx, me]]
    pass_diag(0)
    service(0)
    unpack(0)

    def factor_block(J, carry):
        r0 = pl.multiple_of(J * 128, 128)
        blk[...] = w[pl.ds(r0, 128), pl.ds(r0, 128)]
        for j in range(16):
            if j == 5:

                @pl.when(J == 0)
                def _():
                    for c in range(1, 4):
                        pass_diag(c)

            if j == 8:

                @pl.when(J == 2)
                def _():
                    service(2)

            sweep8(j, blk, ltb)
        for s in range(4):

            @pl.when(J == s)
            def _(s=s):
                if s == 0:
                    for c in range(1, 4):
                        unpack(c)
                block_update(s, w, lt, blk, ltb)
                if s == 0:
                    service(1)
                if s == 3:
                    service(3)

        return carry

    lax.fori_loop(0, 4, factor_block, 0)

    pick = lax.broadcasted_iota(jnp.int32, (8, 512), 1) == me * 8 + lax.broadcasted_iota(jnp.int32, (8, 512), 0)
    factor_ref[...] = dot32(pick.astype(jnp.float32), lt[...], tb=True)
    own = zg[:, pl.ds(z, 1)].reshape(TILES * SLAB, WIDTH)
    wv = w[...]
    solved_ref[...] = dot48(own, wv, tb=True).reshape(TILES, SLAB, WIDTH)
    lt[...] = dot48(wv.T, wv)
    for t in range(TILES):
        bhi[t], blo[t] = split(dot48(zg[t].reshape(TW, WIDTH), lt[...]))

    for c in trail_in:
        c.start()
    for pos in (0, 1, 4, 2, 5, 3, 6, 7):
        yy = (y + step_of[pos]) % 8
        remote(sb.at[:, 0], sb.at[:, 0], sb_s, sb_r.at[pos], dev(dx=1)).wait_recv()
        back = (-step_of[pos]) % 8
        if back == 0:
            sa_copy(0).wait_recv()
        else:
            remote(pa.at[0], pa.at[0], sa_s, sa_r.at[back], dev(dy=1)).wait_recv()

        def convert(i, c, yy=yy):
            v = jnp.concatenate([pb[i // 2, i % 2, yy], pa[yy, i % 2, i // 2]], axis=0)
            hi, lo = split(v)
            at = (i // 2 * 8 + yy) * 2 + i % 2
            ph[at] = hi
            pll[at] = lo
            return c

        lax.fori_loop(0, 8, convert, 0)

    loads[7].wait()
    for t in range(TILES):
        live, hi, lo = [], [], []
        for s in range(SLOTS):
            p = slots_s[t, s, me]
            live.append((p >= 0).astype(jnp.float32))
            src = jnp.maximum(p, 0) // TILES
            hi.append(ph[src])
            lo.append(pll[src])
        hi, lo = jnp.concatenate(hi, axis=0), jnp.concatenate(lo, axis=0)
        bh, bl = bhi[t], blo[t]
        upd = dot16(hi, bh) + (dot16(hi, bl) + dot16(lo, bh))
        trail_in[t].wait()
        for s in range(SLOTS):
            out_v[t, s] = trail_v[t, s] - upd[s * SLAB : s * SLAB + SLAB] * live[s]
        trail_out[t].start()

    for c in range(4):

        @pl.when(x >= c)
        def _(c=c):
            dy_all(c).wait_send()
            dx_all(c).wait_send()

        dk_copy(c).wait_send()
    xa_all.wait_send()
    for step in range(4):
        for way in range(2):
            z_copy(step, way).wait_send()
            y_copy(step, way).wait_send()
    remote(sb, sb, sb_s, sb_r.at[0], dev(dx=1)).wait_send()
    remote(sa, sa, sa_s, sa_r.at[0], dev(dy=1)).wait_send()
    for c in trail_out:
        c.wait()


def deliver(factor_ref, solved_ref, trail_ref, factor_out, solved_out, trail_out, fv, sv, tv, i_sem, o_sem):
    stages = [(trail_ref.at[t], tv.at[t], trail_out.at[t]) for t in range(TILES)]
    stages += [(solved_ref, sv, solved_out), (factor_ref, fv, factor_out)]
    come = [pltpu.make_async_copy(a, b, i_sem.at[n]) for n, (a, b, _) in enumerate(stages)]
    leave = [pltpu.make_async_copy(b, c, o_sem.at[n]) for n, (_, b, c) in enumerate(stages)]
    for c in come:
        c.start()
    for a, b in zip(come, leave):
        a.wait()
        b.start()
    for c in leave:
        c.wait()


def per_device(diag_block, panel, panel_mask, slot_rows, trail):
    f32, i32 = jnp.float32, jnp.int32
    vm = lambda *shape: pltpu.VMEM(shape, f32)
    dma = lambda *shape: pltpu.SemaphoreType.DMA(shape)
    one = pltpu.SemaphoreType.DMA
    vmem = pl.BlockSpec(memory_space=pltpu.VMEM)
    hbm = pl.BlockSpec(memory_space=pl.ANY)
    shapes = (
        jax.ShapeDtypeStruct(diag_block.shape, f32),
        jax.ShapeDtypeStruct(panel.shape, f32),
        jax.ShapeDtypeStruct(trail.shape, f32),
    )
    slots = jnp.transpose(slot_rows, (1, 2, 0))
    bf = lambda *shape: pltpu.VMEM(shape, jnp.bfloat16)
    results = pl.pallas_call(
        kernel,
        out_shape=shapes,
        in_specs=[hbm] * 5,
        out_specs=(vmem, vmem, hbm),
        scratch_shapes=[
            vm(4, NK, NX, NY, 8, 128), vm(512, 512), vm(512, 512), vm(128, 128), vm(128, 128),
            vm(NX, TILES, RA, WIDTH), vm(TILES, NZ, SLAB, WIDTH),
            *[vm(TILES, RB, WIDTH) for _ in range(8)],
            vm(7, 8, RB, WIDTH), vm(15, NX, RA, WIDTH),
            vm(NX, NK, NY, RB, WIDTH), vm(NY, NK, NX, RA, WIDTH),
            bf(TILES, TW, WIDTH), bf(TILES, TW, WIDTH), bf(64, SLAB, WIDTH), bf(64, SLAB, WIDTH),
            vm(TILES, SLOTS, SLAB, TW), vm(TILES, SLOTS, SLAB, TW),
            vm(TILES, SLAB, WIDTH), pltpu.VMEM((2, TILES), i32), pltpu.VMEM(slots.shape, i32),
            pltpu.SMEM(slots.shape, i32), pltpu.VMEM((16, 64), i32), pltpu.SMEM((16, 64), i32),
            dma(4), dma(4), dma(4), dma(4, 3), dma(4), dma(4), one, one,
            dma(4, 2), dma(4, 2), dma(4, 2), dma(4, 2), one, dma(8), one, dma(8),
            dma(9), dma(4), dma(4),
        ],
        compiler_params=pltpu.CompilerParams(
            collective_id=0, has_side_effects=True, vmem_limit_bytes=58 * 1024 * 1024
        ),
        name="panels",
    )(diag_block, panel, panel_mask.T, slots, trail)
    return pl.pallas_call(
        deliver,
        out_shape=shapes,
        in_specs=[hbm] * 3,
        out_specs=(hbm,) * 3,
        scratch_shapes=[vm(*diag_block.shape), vm(*panel.shape), vm(*trail.shape), dma(6), dma(6)],
        compiler_params=pltpu.CompilerParams(vmem_limit_bytes=58 * 1024 * 1024),
        name="deliver",
    )(*results)


def solution(mesh):
    in_specs = (
        P("row", None),
        P("row", "col", None),
        P("row", None),
        P(),
        P("row", None, "col", None),
    )
    out_specs = (P("row", None), P("row", "col", None), P("row", None, "col", None))
    return jax.shard_map(
        per_device, mesh=mesh, in_specs=in_specs, out_specs=out_specs, check_vma=False
    )
```

time: 97.4 us -> 75.5 us (0.78)
  Pallas kernels: 84.4 us -> 74.7 us
  local copies, waits for them, and re-layouts: 9.2 us -> 0 us
  other arithmetic: 2.79 us -> 0 us
    pallas_call x1 -> x2, Pallas kernels: 84.4 us -> 74.7 us  [the longest x1 72.1 us: per_device(): pl.pallas_call(kernel, out_shape=shapes, in_specs=[hbm] * 5, out_specs=(v...]
    unnamed x4 -> x0, local copies, waits for them, and re-layouts: 7.49 us -> none
    reduce_max x1 -> x0, other arithmetic: 2.03 us -> none  [per_device(): table = jnp.max(jnp.where(match, (slots & 3)[:, :, None], 0), axis=1)]
    dynamic_slice x1 -> x0, local copies, waits for them, and re-layouts: 1.56 us -> none  [per_device(): my_slots = lax.dynamic_index_in_dim(slot_rows, me, 0, keepdims=False)]
where the time goes in v1:
time: 75.5 us; the launch traced here: 75.3 us
  Pallas kernels  74.7 us (99%)
    pallas_call x1, Pallas kernels, per_device(): pl.pallas_call(kernel, out_shape=shapes, in_specs=[hbm] * 5, out_specs=(v...  72.1 us
    pallas_call x1, Pallas kernels, per_device(): pl.pallas_call(deliver, out_shape=shapes, in_specs=[hbm] * 3, out_specs=(...  2.54 us

profile of v1, /device:TPU:1, one launch (start us, length us, event | category | flops | bytes accessed | tf_op | source)
XLA Modules:
  0.0 75.3 jit_solution(13053401712490686049)
XLA Ops:
  0.6 72.1 %panels.1 = (f32[8,512]{1,0:T(8,128)}, f32[4,32,512]{2,1,0:T(8,128)}, f32[4,16,32,256]{3,2,1,0:T(8,128)}) custom-call(f32[8,512]{1,0:T(8,128)} %diag_ref.1, f32[4,32,512]{2,1,0:T(8,128)} %panel_ref.1, s32[2,4]{1,0:T(2,128)} %bitcast.3, s32[4,16,64]{2,1,0:T(8,128)} %bitcast.2, f32[4,16,32,256]{3,2,1,0:T(8,128)} %trail_ref.1), custom_call_target="tpu_custom_call" | custom-call | tf_op jit(solution)/shard_map/panels/pallas_call | solution.py:475
  72.7 2.5 %deliver.1 = (f32[8,512]{1,0:T(8,128)}, f32[4,32,512]{2,1,0:T(8,128)}, f32[4,16,32,256]{3,2,1,0:T(8,128)}) custom-call(f32[8,512]{1,0:T(8,128)} %get-tuple-element.6.factor_ref, f32[4,32,512]{2,1,0:T(8,128)} %get-tuple-element.7.solved_ref, f32[4,16,32,256]{3,2,1,0:T(8,128)} %get-tuple-element.8.trail_ref), custom_call_target="tpu_custom_call" | custom-call | tf_op jit(solution)/shard_map/deliver/pallas_call | solution.py:499

commit v2 on v1

--- a/solution.py
+++ b/solution.py
@@ -11,6 +11,8 @@
 TILES, SLAB, WIDTH, TW = 4, 32, 512, 256
 RB, RA = 24, 8
 SLOTS = 16
+SCHEDULE = {(0, 10): (("y", 1),), (0, 16): (("z", 1),), (1, 10): (("y", 2),), (1, 16): (("z", 2),), (2, 8): (("y", 3),), (2, 16): (("z", 3),)}
+CUTS = (4, 8, 12, 15)
 
 
 def dot32(a, b, tb=False):
@@ -277,14 +279,19 @@
 
         lax.fori_loop(0, 7, body, 0)
 
+    def sa_to(e):
+        m = (e + 1) // 2
+        d = (m + 1) // 2
+        return (8 + d * (2 * (m % 2) - 1)) % 8, (e + 1) % 2
+
     def sa_copy(e):
-        return remote(
-            sa.at[e], pa.at[y, k], sa_s, sa_r.at[(e + 1) // 2], dev(dy=(e + 1) // 2, dk=(e + 1) % 2)
-        )
+        dy, dk = sa_to(e)
+        return remote(sa.at[e], pa.at[y, k], sa_s, sa_r.at[dy], dev(dy=dy, dk=dk))
 
     def send_cross(lo, hi):
         def body(e, c):
-            to = dev(dy=(e + 1) // 2, dk=(e + 1) % 2)[0]
+            dy, dk = sa_to(e)
+            to = dev(dy=dy, dk=dk)[0]
             for xx in range(NX):
                 sa[e, xx] = xa[xx, table_s[8 + xx, to]]
             sa_copy(e).start()
@@ -292,21 +299,22 @@
 
         lax.fori_loop(lo, hi, body, 0)
 
-    def service(step):
+    def service_y(step):
         for way in range(2):
             y_copy(step, way).wait_recv()
             if step < 3:
                 y_copy(step + 1, way).start()
-        for way in range(2):
-            z_copy(step, way).wait_recv()
-            if step < 3:
-                z_copy(step + 1, way).start()
         if step < 3:
             send_block(step + 1)
             send_block(step + 4)
         else:
             send_block(7)
-        send_cross(4 * step, min(4 * step + 4, 15))
+
+    def service_z(step):
+        for way in range(2):
+            z_copy(step, way).wait_recv()
+            if step < 3:
+                z_copy(step + 1, way).start()
 
     def turn_diag(c):
         @pl.when(x >= c)
@@ -330,18 +338,29 @@
             v = jnp.stack([a7[c, 0, xx], a7[c, 1, xx]], axis=1)
             w[xx * 128 : xx * 128 + 128, c * 128 : c * 128 + 128] = v.reshape(128, 128)
 
+    to_scalar.wait()
+    send_block(0)
+    turn_diag(0)
+    xa_all.wait_recv()
+    for c in range(1, 4):
+        turn_diag(c)
+    for xx in range(NX):
+        pa[y, k, xx] = xa[xx, table_s[8 + xx, me]]
     w[...] = jnp.zeros_like(w)
     lt[...] = jnp.zeros_like(lt)
-    for c in range(4):
-        turn_diag(c)
-    to_scalar.wait()
-    send_block(0)
-    xa_all.wait_recv()
-    for xx in range(NX):
-        pa[y, k, xx] = xa[xx, table_s[8 + xx, me]]
+    service_y(0)
+    send_cross(0, CUTS[0])
     pass_diag(0)
-    service(0)
+    service_z(0)
     unpack(0)
+
+    def serve(what):
+        for axis, step in what:
+            if axis == "y":
+                service_y(step)
+                send_cross(CUTS[step - 1], CUTS[step])
+            else:
+                service_z(step)
 
     def factor_block(J, carry):
         r0 = pl.multiple_of(J * 128, 128)
@@ -354,11 +373,12 @@
                     for c in range(1, 4):
                         pass_diag(c)
 
-            if j == 8:
-
-                @pl.when(J == 2)
-                def _():
-                    service(2)
+            for s in range(4):
+                if (s, j) in SCHEDULE:
+
+                    @pl.when(J == s)
+                    def _(s=s, j=j):
+                        serve(SCHEDULE[s, j])
 
             sweep8(j, blk, ltb)
         for s in range(4):
@@ -369,10 +389,7 @@
                     for c in range(1, 4):
                         unpack(c)
                 block_update(s, w, lt, blk, ltb)
-                if s == 0:
-                    service(1)
-                if s == 3:
-                    service(3)
+                serve(SCHEDULE.get((s, 16), ()))
 
         return carry
 

time: 75.5 us -> 70.3 us (0.931)
  Pallas kernels: 74.7 us -> 69.5 us
    pallas_call x1, Pallas kernels: 72.1 us -> 67 us  [per_device(): pl.pallas_call(kernel, out_shape=shapes, in_specs=[hbm] * 5, out_specs=(v...]
where the time goes in v2:
time: 70.3 us; the launch traced here: 70.1 us
  Pallas kernels  69.5 us (99%)
    pallas_call x1, Pallas kernels, per_device(): pl.pallas_call(kernel, out_shape=shapes, in_specs=[hbm] * 5, out_specs=(v...  67 us
    pallas_call x1, Pallas kernels, per_device(): pl.pallas_call(deliver, out_shape=shapes, in_specs=[hbm] * 3, out_specs=(...  2.54 us

profile of v2, /device:TPU:1, one launch (start us, length us, event | category | flops | bytes accessed | tf_op | source)
XLA Modules:
  0.0 70.1 jit_solution(2896291315059359417)
XLA Ops:
  0.6 67.0 %panels.1 = (f32[8,512]{1,0:T(8,128)}, f32[4,32,512]{2,1,0:T(8,128)}, f32[4,16,32,256]{3,2,1,0:T(8,128)}) custom-call(f32[8,512]{1,0:T(8,128)} %diag_ref.1, f32[4,32,512]{2,1,0:T(8,128)} %panel_ref.1, s32[2,4]{1,0:T(2,128)} %bitcast.3, s32[4,16,64]{2,1,0:T(8,128)} %bitcast.2, f32[4,16,32,256]{3,2,1,0:T(8,128)} %trail_ref.1), custom_call_target="tpu_custom_call" | custom-call | tf_op jit(solution)/shard_map/panels/pallas_call | solution.py:492
  67.6 2.5 %deliver.1 = (f32[8,512]{1,0:T(8,128)}, f32[4,32,512]{2,1,0:T(8,128)}, f32[4,16,32,256]{3,2,1,0:T(8,128)}) custom-call(f32[8,512]{1,0:T(8,128)} %get-tuple-element.6.factor_ref, f32[4,32,512]{2,1,0:T(8,128)} %get-tuple-element.7.solved_ref, f32[4,16,32,256]{3,2,1,0:T(8,128)} %get-tuple-element.8.trail_ref), custom_call_target="tpu_custom_call" | custom-call | tf_op jit(solution)/shard_map/deliver/pallas_call | solution.py:516

commit v3 on v2

--- a/solution.py
+++ b/solution.py
@@ -23,6 +23,10 @@
 def dot16(a, b):
     dims = (((1,), (1,)), ((), ()))
     return lax.dot_general(a, b, dims, preferred_element_type=jnp.float32)
+
+
+def dot_nn(a, b):
+    return lax.dot_general(a, b, (((1,), (0,)), ((), ())), preferred_element_type=jnp.float32)
 
 
 def split(x):
@@ -132,7 +136,7 @@
 def kernel(
     diag_ref, panel_ref, mask_ref, slots_ref, trail_ref,
     factor_ref, solved_ref, out_ref,
-    a7, w, lt, blk, ltb, xa, zg, yb0, yb1, yb2, yb3, yb4, yb5, yb6, yb7,
+    a7, w, lt, blk, ltb, turn, avh, avl, xa, zg, yb0, yb1, yb2, yb3, yb4, yb5, yb6, yb7,
     sb, sa, pb, pa, bhi, blo, ph, pll, trail_v, out_v, panel_v, mask_v, slots_v, slots_s, table_v, table_s,
     dy_s, dy_r, dx_s, dx_r, dk_s, dk_r, xa_s, xa_r, z_s, z_r, y_s, y_r, sb_s, sb_r, sa_s, sa_r, l_sem, t_sem, o_sem,
 ):
@@ -271,7 +275,8 @@
         buf = yb[pos]
         pb[x, k, yy] = buf[table_s[yy, me]]
 
-        def body(e, c):
+        def body(i, c):
+            e = (i + 3) % 7
             to = dev(dx=(e + 1) // 2, dk=(e + 1) % 2)[0]
             sb[e, pos] = buf[table_s[yy, to]]
             sb_copy(pos, e, yy).start()
@@ -350,8 +355,8 @@
     lt[...] = jnp.zeros_like(lt)
     service_y(0)
     send_cross(0, CUTS[0])
+    service_z(0)
     pass_diag(0)
-    service_z(0)
     unpack(0)
 
     def serve(what):
@@ -395,14 +400,19 @@
 
     lax.fori_loop(0, 4, factor_block, 0)
 
-    pick = lax.broadcasted_iota(jnp.int32, (8, 512), 1) == me * 8 + lax.broadcasted_iota(jnp.int32, (8, 512), 0)
-    factor_ref[...] = dot32(pick.astype(jnp.float32), lt[...], tb=True)
+    wv = w[...]
+    wh, wl = split(wv)
+    th, tl = split(wv.T)
+    ainv = dot_nn(th, wh) + (dot_nn(th, wl) + dot_nn(tl, wh))
+    avh[...], avl[...] = split(ainv)
+    for t in range(TILES):
+        qh, ql = split(zg[t].reshape(TW, WIDTH))
+        bhi[t], blo[t] = split(dot_nn(qh, avh[...]) + (dot_nn(qh, avl[...]) + dot_nn(ql, avh[...])))
+
+    turn[...] = lt[:, pl.ds(pl.multiple_of(me // 16 * 128, 128), 128)].T
+    factor_ref[...] = turn[pl.ds(pl.multiple_of(me % 16 * 8, 8), 8), :]
     own = zg[:, pl.ds(z, 1)].reshape(TILES * SLAB, WIDTH)
-    wv = w[...]
-    solved_ref[...] = dot48(own, wv, tb=True).reshape(TILES, SLAB, WIDTH)
-    lt[...] = dot48(wv.T, wv)
-    for t in range(TILES):
-        bhi[t], blo[t] = split(dot48(zg[t].reshape(TW, WIDTH), lt[...]))
+    solved_ref[...] = dot48(own, w[...], tb=True).reshape(TILES, SLAB, WIDTH)
 
     for c in trail_in:
         c.start()
@@ -496,6 +506,7 @@
         out_specs=(vmem, vmem, hbm),
         scratch_shapes=[
             vm(4, NK, NX, NY, 8, 128), vm(512, 512), vm(512, 512), vm(128, 128), vm(128, 128),
+            vm(128, 512), bf(512, 512), bf(512, 512),
             vm(NX, TILES, RA, WIDTH), vm(TILES, NZ, SLAB, WIDTH),
             *[vm(TILES, RB, WIDTH) for _ in range(8)],
             vm(7, 8, RB, WIDTH), vm(15, NX, RA, WIDTH),

time: 70.3 us -> 70.3 us (level)
  no operation moved by 1% of the time
where the time goes in v3:
time: 70.3 us; the launch traced here: 70.1 us
  Pallas kernels  69.5 us (99%)
    pallas_call x1, Pallas kernels, per_device(): pl.pallas_call(kernel, out_shape=shapes, in_specs=[hbm] * 5, out_specs=(v...  67 us
    pallas_call x1, Pallas kernels, per_device(): pl.pallas_call(deliver, out_shape=shapes, in_specs=[hbm] * 3, out_specs=(...  2.54 us

profile of v3, /device:TPU:1, one launch (start us, length us, event | category | flops | bytes accessed | tf_op | source)
XLA Modules:
  0.0 70.1 jit_solution(13227266007411911119)
XLA Ops:
  0.6 67.0 %panels.1 = (f32[8,512]{1,0:T(8,128)}, f32[4,32,512]{2,1,0:T(8,128)}, f32[4,16,32,256]{3,2,1,0:T(8,128)}) custom-call(f32[8,512]{1,0:T(8,128)} %diag_ref.1, f32[4,32,512]{2,1,0:T(8,128)} %panel_ref.1, s32[2,4]{1,0:T(2,128)} %bitcast.3, s32[4,16,64]{2,1,0:T(8,128)} %bitcast.2, f32[4,16,32,256]{3,2,1,0:T(8,128)} %trail_ref.1), custom_call_target="tpu_custom_call" | custom-call | tf_op jit(solution)/shard_map/panels/pallas_call | solution.py:502
  67.6 2.5 %deliver.1 = (f32[8,512]{1,0:T(8,128)}, f32[4,32,512]{2,1,0:T(8,128)}, f32[4,16,32,256]{3,2,1,0:T(8,128)}) custom-call(f32[8,512]{1,0:T(8,128)} %get-tuple-element.6.factor_ref, f32[4,32,512]{2,1,0:T(8,128)} %get-tuple-element.7.solved_ref, f32[4,16,32,256]{3,2,1,0:T(8,128)} %get-tuple-element.8.trail_ref), custom_call_target="tpu_custom_call" | custom-call | tf_op jit(solution)/shard_map/deliver/pallas_call | solution.py:527
